TPU v7x, 128 devices: a whole 4x4x4 slice. The times are simulated.
128 devices in a mesh: expert: 4 (over x), row: 16 (over z, y), col: 2 (over core).
Axes of the slice: x: 4, y: 4, z: 4, core: 2. Of those that a mesh axis runs over, the one named last changes fastest.
Arguments:
- tokens: bfloat16 [8192, 4096], P(('expert', 'row'), 'col'), may hold values from -6 to 6
- router: bfloat16 [4096, 4], P('col'), may hold values from -0.09375 to 0.09375
- up_weight: bfloat16 [4, 4096, 14336], P('expert', 'col', 'row'), may hold values from -0.09375 to 0.09375
- down_weight: bfloat16 [4, 14336, 4096], P('expert', 'row', 'col'), may hold values from -0.046875 to 0.046875
- choices: int32 [64, 4, 8], P(('expert', 'row')), may hold values from -1 to 127, as said below
Outputs:
- mixed: bfloat16 [8192, 4096], P(('expert', 'row'), 'col')
Inputs may be any that keep to these rules, and one draw needn't show every extreme that they name: `choices`: entry [s, e] lists, as local rows of source block s's 128 tokens, the tokens that expert e chooses from that block, distinct and ascending, followed by -1 padding. Each expert chooses exactly 384 tokens in all; from one block it chooses at least 4 and at most 8, and for every expert some block fills all 8 slots.
All inputs are finite; a program needn't handle non-finite values.
Results may differ from a plain program's by a relative error of at most 0.02.
Values may be sent and summed in bfloat16 or wider, within the bound.
No kernel may reach another device: no remote copies, remote signals or barrier semaphores. Data moves between devices by JAX's collectives and lax.ppermute only.
A program may use at most 64 MiB of HBM per device.

v0:
```python
import functools

import jax
import jax.numpy as jnp
from jax import lax
from jax.experimental import pallas as pl
from jax.experimental.pallas import tpu as pltpu
from jax.sharding import PartitionSpec as P

SIDE = 4
QUARTERS = 4
BAND = 128
PER_SRC = 6
EMPTY = 8.0
VMEM = 16 * 1024 * 1024
A, B, LEFT, RIGHT = ("own", 1), ("own", 3), ("other", 1), ("other", 3)
CHANGE = {A: 1, B: 3, LEFT: 2, RIGHT: 2}
DISPATCH = ((B, LEFT, 0, 8), (A, A, 0, 8), (LEFT, B, 0, 8))
RETURN = DISPATCH


def pairs_of(move):
    pairs = []
    for z in range(SIDE):
        for y in range(SIDE):
            for core in range(2):
                axis, flip = move[core]
                along_y = (axis == "own") == (core == 0)
                to = (z * SIDE + (y ^ flip)) if along_y else ((z ^ flip) * SIDE + y)
                pairs.append(((z * SIDE + y) * 2 + core, to * 2 + core))
    return pairs


def class_of(mine_ref, core_ref, move):
    change = [CHANGE[kind] for kind in move[:2]]
    if change[0] == change[1]:
        return mine_ref[0] ^ change[0]
    return mine_ref[0] ^ jnp.where(core_ref[0] == 0, change[0], change[1])


def slot_row(choices):
    experts, slots = choices.shape
    lane = lax.broadcasted_iota(jnp.int32, (slots, experts * slots), 1)
    slot = lax.broadcasted_iota(jnp.int32, (slots, experts * slots), 0)
    tile = (lane % slots == slot).astype(jnp.float32)
    spread = jnp.dot(choices.astype(jnp.float32), tile, preferred_element_type=jnp.float32)
    lane = lax.broadcasted_iota(jnp.int32, spread.shape, 1)
    expert = lax.broadcasted_iota(jnp.int32, spread.shape, 0)
    row = jnp.sum(jnp.where(lane // slots == expert, spread, 0.0), axis=0, keepdims=True)
    return row.astype(jnp.int32)


def one_hot(ids, local_tokens):
    return lax.broadcasted_iota(jnp.int32, (local_tokens, ids.shape[1]), 0) == ids


def spread_kernel(core_ref, picked_ref, hot_ref, out_ref):
    slots, quarter = out_ref.shape[1:]
    experts = out_ref.shape[0] // (SIDE * SIDE)
    live = jnp.sum(hot_ref[...].astype(jnp.float32), axis=1, keepdims=True)
    mark = jnp.broadcast_to((1.0 - live) * EMPTY, (experts * slots, 128))
    core = core_ref[0]
    parts = []
    for q in range(QUARTERS):
        part = picked_ref[:, q * quarter : (q + 1) * quarter]
        part = jnp.concatenate([part[:, :128] + mark, part[:, 128:]], axis=1)
        parts.append(part.reshape(experts, slots, quarter).astype(jnp.bfloat16))
    for a in range(SIDE):
        for b in range(SIDE):
            k0, k1 = (b + 2 * a) % QUARTERS, (a + 2 * b) % QUARTERS
            value = parts[k0] if k0 == k1 else jnp.where(core == 0, parts[k0], parts[k1])
            for e in range(experts):
                out_ref[e * SIDE * SIDE + a * SIDE + b] = value[e]


def compact_kernel(x_ref, full_ref, where_ref):
    rows = x_ref.shape[0]
    capacity = full_ref.shape[0]
    live = (x_ref[:, :128].astype(jnp.float32) < EMPTY - 1.0).astype(jnp.bfloat16)
    i = lax.broadcasted_iota(jnp.int32, (rows, rows), 0)
    j = lax.broadcasted_iota(jnp.int32, (rows, rows), 1)
    contract = (((0,), (0,)), ((), ()))
    upto = lax.dot_general(
        live, (i <= j).astype(jnp.bfloat16), contract, preferred_element_type=jnp.float32
    )[:8]
    before = jnp.where(j[:8] == 0, 0.0, pltpu.roll(upto, 1, 1))
    position = jnp.where(upto > before, before, -1.0).astype(jnp.int32)[:1]
    for p in range(0, capacity, BAND):
        columns = slice(p, p + 2 * BAND)
        target = lax.broadcasted_iota(jnp.int32, (BAND, 2 * BAND), 0) + p
        where = (target == position[:, columns]).astype(jnp.bfloat16)
        where_ref[p : p + BAND, :] = where
        full_ref[p : p + BAND, :] = jnp.dot(
            where, x_ref[columns, :], preferred_element_type=jnp.float32
        ).astype(jnp.bfloat16)


def up_product(where, rows_ref, up_ref):
    quarter = rows_ref.shape[1]
    start = pl.multiple_of(where * quarter, quarter)
    return jnp.dot(
        rows_ref[...], up_ref[pl.ds(start, quarter), :], preferred_element_type=jnp.float32
    )


def first_up_kernel(mine_ref, core_ref, rows_ref, up_ref, out_ref):
    out_ref[...] = up_product(mine_ref[0], rows_ref, up_ref)


def next_up_kernel(move, mine_ref, core_ref, sum_ref, rows_ref, up_ref, out_ref):
    at = class_of(mine_ref, core_ref, move)
    out_ref[...] = sum_ref[...] + up_product(at, rows_ref, up_ref)


def last_up_kernel(move, mine_ref, core_ref, sum_ref, rows_ref, up_ref, out_ref, send_ref):
    at = class_of(mine_ref, core_ref, move)
    total = sum_ref[...] + up_product(at, rows_ref, up_ref)
    out_ref[...] = total
    send_ref[...] = total.astype(jnp.bfloat16)


def down_kernel(mine_ref, core_ref, sum_ref, other_ref, down_ref, hidden_ref, *out_refs):
    rows = hidden_ref.shape[0]
    block = rows // 2
    for i in range(2):
        at = slice(i * block, (i + 1) * block)
        value = sum_ref[at, :] + other_ref[at, :].astype(jnp.float32)
        hidden = jax.nn.gelu(value, approximate=True).astype(jnp.bfloat16)
        hidden_ref[at, :] = hidden
        for move, out_ref in zip(RETURN, out_refs):
            first, last = move[2:]
            eighth = out_ref.shape[1] // (last - first)
            start = (class_of(mine_ref, core_ref, move) * 8 + first) * eighth
            columns = pl.ds(pl.multiple_of(start, 2 * eighth), out_ref.shape[1])
            out_ref[at, :] = jnp.dot(
                hidden, down_ref[:, columns], preferred_element_type=jnp.float32
            ).astype(jnp.bfloat16)


def own_down_kernel(mine_ref, hidden_ref, down_ref, where_ref, out_ref, turned_ref):
    quarter = out_ref.shape[1]
    start = pl.multiple_of(mine_ref[0] * quarter, quarter)
    out_ref[...] = jnp.dot(
        hidden_ref[...], down_ref[:, pl.ds(start, quarter)], preferred_element_type=jnp.float32
    )
    for p in range(0, where_ref.shape[0], BAND):
        where = where_ref[p : p + BAND, :].astype(jnp.float32)
        turned_ref[p : p + BAND, BAND:] = where[:, :BAND].T.astype(jnp.bfloat16)
        turned_ref[p + BAND : p + 2 * BAND, :BAND] = where[:, BAND:].T.astype(jnp.bfloat16)


def return_kernel(own_ref, *refs):
    *piece_refs, turned_ref, out_ref = refs
    total = own_ref[...]
    for piece_ref in piece_refs:
        total += piece_ref[...].astype(jnp.float32)
    total = total.astype(jnp.bfloat16)
    for row in range(0, out_ref.shape[0], BAND):
        low, high = max(row - BAND, 0), min(row + BAND, total.shape[0])
        columns = slice(low - row + BAND, high - row + BAND)
        out_ref[row : row + BAND, :] = jnp.dot(
            turned_ref[row : row + BAND, columns], total[low:high], preferred_element_type=jnp.float32
        ).astype(jnp.bfloat16)


def weight_kernel(choices_ref, logits_ref, other_ref, out_ref):
    experts, slots = choices_ref.shape[1:]
    local_tokens = logits_ref.shape[0]
    ids = slot_row(choices_ref[0])
    gates = jax.nn.sigmoid(logits_ref[...] + other_ref[...])
    lane = lax.broadcasted_iota(jnp.int32, (local_tokens, experts * slots), 1)
    weights = jnp.zeros((local_tokens, experts * slots), jnp.float32)
    for e in range(experts):
        weights = jnp.where(lane // slots == e, gates[:, e : e + 1], weights)
    weights = jnp.where(one_hot(ids, local_tokens), weights, 0.0)
    high = weights.astype(jnp.bfloat16)
    low = (weights - high.astype(jnp.float32)).astype(jnp.bfloat16)
    out_ref[...] = jnp.concatenate([high, low], axis=1)


def mix_kernel(core_ref, arrived_ref, weights_ref, out_hbm, out_ref, sems):
    slots, quarter = arrived_ref.shape[1:]
    experts = arrived_ref.shape[0] // (SIDE * SIDE)
    weights = weights_ref[...]
    core = core_ref[0]
    stores = []
    for q in range(QUARTERS):
        total = []
        for e in range(experts):
            part = jnp.zeros((slots, quarter), jnp.float32)
            for a in range(SIDE):
                b = (q - 2 * a) % QUARTERS
                at = jnp.where(core == 0, a * SIDE + b, b * SIDE + a)
                part += arrived_ref[e * SIDE * SIDE + at].astype(jnp.float32)
            total.append(part)
        total = jnp.concatenate(total + total, axis=0).astype(jnp.bfloat16)
        mixed = jnp.dot(weights, total, preferred_element_type=jnp.float32)
        at = pl.ds(q * quarter, quarter)
        out_ref[:, at] = mixed.astype(jnp.bfloat16)
        stores.append(pltpu.make_async_copy(out_ref.at[:, at], out_hbm.at[:, at], sems.at[q]))
        stores[-1].start()
    for store in stores:
        store.wait()


def call(kernel, scalars, arrays, outs, scratch=(), space=pltpu.VMEM):
    vmem = lambda: pl.BlockSpec(memory_space=pltpu.VMEM)
    return pl.pallas_call(
        kernel,
        out_shape=outs,
        in_specs=[pl.BlockSpec(memory_space=pltpu.SMEM) for _ in scalars]
        + [vmem() for _ in arrays],
        out_specs=jax.tree.map(lambda _: pl.BlockSpec(memory_space=space), outs),
        scratch_shapes=list(scratch),
        compiler_params=pltpu.CompilerParams(vmem_limit_bytes=VMEM),
    )(*scalars, *arrays)


def on_device(tokens, router, up_weight, down_weight, choices):
    n_expert = lax.axis_size("expert")
    n_row = lax.axis_size("row")
    sources = n_expert * n_row
    slots = choices.shape[2]
    local_tokens, width = tokens.shape
    quarter = width // QUARTERS
    capacity = PER_SRC * sources
    swap = [(0, 1), (1, 0)]
    core = lax.axis_index("col")
    row = lax.axis_index("row")
    z, y = row // SIDE, row % SIDE
    mine = jnp.where(core == 0, y + 2 * z, z + 2 * y) % QUARTERS
    core_at = core.astype(jnp.int32).reshape(1)
    up_local = up_weight[0]
    down_local = down_weight[0]

    mine_at = mine.astype(jnp.int32).reshape(1)
    place = [mine_at, core_at]
    hidden_units = up_local.shape[1]

    def shape(*dims, dtype=jnp.bfloat16):
        return jax.ShapeDtypeStruct(dims, dtype)

    def send(array, move):
        return lax.ppermute(array, ("row", "col"), pairs_of(move))

    token_rows = jnp.arange(local_tokens, dtype=jnp.int32)
    hot = (choices[0][:, :, None] == token_rows).astype(jnp.bfloat16)
    hot = hot.reshape(n_expert * slots, local_tokens)
    picked = jnp.dot(hot, tokens, preferred_element_type=jnp.float32)
    spread = call(spread_kernel, [core_at], [picked, hot], shape(sources, slots, quarter))
    own = lax.all_to_all(spread, ("expert", "row"), split_axis=0, concat_axis=0, tiled=True)
    full, where = call(
        compact_kernel,
        [],
        [own.reshape(sources * slots, quarter)],
        (shape(capacity, quarter), shape(capacity, 2 * BAND)),
    )
    pieces = [send(full, move) for move in DISPATCH]

    sums = shape(capacity, hidden_units, dtype=jnp.float32)
    up_part = call(first_up_kernel, place, [full, up_local], sums)
    for move, piece in zip(DISPATCH[:-1], pieces):
        kernel = functools.partial(next_up_kernel, move)
        up_part = call(kernel, place, [up_part, piece, up_local], sums)
    up_part, rounded = call(
        functools.partial(last_up_kernel, DISPATCH[-1]),
        place,
        [up_part, pieces[-1], up_local],
        (sums, shape(capacity, hidden_units)),
    )
    other = lax.ppermute(rounded, "col", swap)

    hidden, *pieces = call(
        down_kernel,
        place,
        [up_part, other, down_local],
        (shape(capacity, hidden_units),)
        + tuple(shape(capacity, quarter // 8 * (last - first)) for _, _, first, last in RETURN),
    )
    pieces = [send(piece, move) for piece, move in zip(pieces, RETURN)]
    own, turned = call(
        own_down_kernel,
        [mine_at],
        [hidden, down_local, where],
        (
            shape(capacity, quarter, dtype=jnp.float32),
            shape(sources * slots, 2 * BAND),
        ),
    )
    late_router, own = lax.optimization_barrier((router, own))
    logits = jnp.dot(tokens, late_router, preferred_element_type=jnp.float32)
    weights = call(
        weight_kernel,
        [],
        [choices, logits, lax.ppermute(logits, "col", swap)],
        shape(local_tokens, 2 * n_expert * slots),
    )
    own, weights = lax.optimization_barrier((own, weights))
    out = call(
        return_kernel,
        [],
        [own, *pieces, turned],
        shape(sources * slots, quarter),
    )
    arrived = lax.all_to_all(
        out.reshape(sources, slots, quarter), ("expert", "row"), split_axis=0, concat_axis=0, tiled=True
    )
    return call(
        mix_kernel,
        [core_at],
        [arrived, weights],
        shape(local_tokens, width),
        scratch=[pltpu.VMEM(tokens.shape, jnp.bfloat16), pltpu.SemaphoreType.DMA((QUARTERS,))],
        space=pl.ANY,
    )


def solution(mesh):
    return jax.shard_map(
        on_device,
        mesh=mesh,
        in_specs=(
            P(("expert", "row"), "col"),
            P("col", None),
            P("expert", "col", "row"),
            P("expert", "row", "col"),
            P(("expert", "row"), None, None),
        ),
        out_specs=P(("expert", "row"), "col"),
        check_vma=False,
    )
```

profile of v0, /device:TPU:0, one launch (start us, length us, event | category | flops | bytes accessed | tf_op | source)
XLA Modules:
  0.0 71.6 jit_solution(6501058199370694343)
XLA Ops:
  0.0 0.0 copy-start
  0.0 0.8 %eq.24 = s32[32]{0:T(128)S(1)} reshape(s32[1,4,8]{2,1,0:T(4,128)} %choices_ref.1) | data formatting | bytes 256 | tf_op jit(solution)/shard_map/eq | solution.py:247
  0.8 0.1 fusion.hot_ref
  0.9 0.2 copy-done
  1.1 0.2 fusion.1.picked_ref
  1.3 0.1 shard_map.55
  1.4 24.4 %all_to_all.10 = bf16[64,8,512]{2,1,0:T(8,128)(2,1)S(1)} all-to-all(bf16[64,8,512]{2,1,0:T(8,128)(2,1)S(1)} %shard_map.55), channel_id=1, replica_groups=mesh['expert'=4,'row'=16,'col'=2] {'expert','row'}, dimensions={0} | all-to-all | bytes 1048576 | tf_op jit(solution)/shard_map/all_to_all | solution.py:251
  25.8 0.5 shard_map.56
  26.4 1.1 %collective-permute-start = (bf16[384,512]{1,0:T(8,128)(2,1)S(1)}, bf16[384,512]{1,0:T(8,128)(2,1)S(1)}, u32[]{:S(2)}, u32[]{:S(2)}) collective-permute-start(bf16[384,512]{1,0:T(8,128)(2,1)S(1)} %get-tuple-element.19.rows_ref), channel_id=1, source_target_pairs={{0,6},{1,3},{2,4},{3,1},{4,2},{5,7},{6,0},{7,5},{8,14},{9,11},{10,... | collective-permute-start | bytes 1179656 | tf_op jit(solution)/shard_map/ppermute | solution.py:244
  27.4 0.3 collective-permute-start.1
  27.8 0.0 collective-permute-start.2
  27.8 0.0 copy-start.1
  27.8 2.0 %copy-done.1 = bf16[1,2048,896]{2,1,0:T(8,128)(2,1)S(1)} copy-done((bf16[1,2048,896]{2,1,0:T(8,128)(2,1)S(1)}, bf16[1,2048,896]{2,1,0:T(8,128)(2,1)}, u32[]{:S(2)}) %copy-start.1) | copy-done | bytes 3670040
  29.8 0.0 copy-start.2
  29.8 0.6 shard_map.57.sum_ref
  30.4 5.1 %collective-permute-done.rows_ref = bf16[384,512]{1,0:T(8,128)(2,1)S(1)} collective-permute-done((bf16[384,512]{1,0:T(8,128)(2,1)S(1)}, bf16[384,512]{1,0:T(8,128)(2,1)S(1)}, u32[]{:S(2)}, u32[]{:S(2)}) %collective-permute-start) | collective-permute-done | bytes 393248 | tf_op jit(solution)/shard_map/ppermute | solution.py:244
  35.4 0.0 copy-done.2
  35.4 0.6 shard_map.58.sum_ref
  36.0 0.0 collective-permute-done.1.rows_ref
  36.0 0.6 shard_map.59.sum_ref
  36.6 0.0 copy-start.3
  36.6 0.0 collective-permute-done.2.rows_ref
  36.6 0.6 shard_map.60
  37.2 0.1 collective-permute-start.3
  37.3 2.1 %collective-permute-done.3.other_ref = bf16[384,896]{1,0:T(8,128)(2,1)S(1)} collective-permute-done((bf16[384,896]{1,0:T(8,128)(2,1)S(1)}, bf16[384,896]{1,0:T(8,128)(2,1)S(1)}, u32[]{:S(2)}, u32[]{:S(2)}) %collective-permute-start.3) | collective-permute-done | bytes 688160 | tf_op jit(solution)/shard_map/ppermute | solution.py:271
  39.5 0.0 copy-done.3
  39.5 1.6 %shard_map.61 = (bf16[384,896]{1,0:T(8,128)(2,1)S(1)}, bf16[384,512]{1,0:T(8,128)(2,1)S(1)}, bf16[384,512]{1,0:T(8,128)(2,1)S(1)}, bf16[384,512]{1,0:T(8,128)(2,1)S(1)}) custom-call(s32[1]{0:T(128)} %bitcast.1.mine_ref, s32[1]{0:T(128)} %bitcast.core_ref, f32[384,896]{1,0:T(8,128)S(1)} %get-tuple-element.20.sum_ref, ...), custom_call_target="tpu_custom_call" | custom-call | tf_op jit(solution)/shard_map/pallas_call | solution.py:208
  41.0 1.5 %collective-permute-start.5 = (bf16[384,512]{1,0:T(8,128)(2,1)S(1)}, bf16[384,512]{1,0:T(8,128)(2,1)S(1)}, u32[]{:S(2)}, u32[]{:S(2)}) collective-permute-start(bf16[384,512]{1,0:T(8,128)(2,1)S(1)} %get-tuple-element.28), channel_id=1, source_target_pairs={{0,6},{1,3},{2,4},{3,1},{4,2},{5,7},{6,0},{7,5},{8,14},{9,11},{10,... | collective-permute-start | bytes 1179656 | tf_op jit(solution)/shard_map/ppermute | solution.py:244
  42.5 0.8 %collective-permute-start.6 = (bf16[384,512]{1,0:T(8,128)(2,1)S(1)}, bf16[384,512]{1,0:T(8,128)(2,1)S(1)}, u32[]{:S(2)}, u32[]{:S(2)}) collective-permute-start(bf16[384,512]{1,0:T(8,128)(2,1)S(1)} %get-tuple-element.29), channel_id=1, source_target_pairs={{0,2},{1,9},{2,0},{3,11},{4,6},{5,13},{6,4},{7,15},{8,10},{9,1},{1... | collective-permute-start | bytes 1179656 | tf_op jit(solution)/shard_map/ppermute | solution.py:244
  43.4 0.5 collective-permute-start.7
  43.9 0.0 copy-start.5
  43.9 0.0 copy-start.4
  43.9 0.6 shard_map.62
  44.4 0.1 copy-done.5
  44.6 0.3 convolution_bitcast_fusion.logits_ref
  44.9 0.1 collective-permute-start.4
  45.0 1.2 %collective-permute-done.4.other_ref = f32[128,4]{1,0:T(8,128)S(1)} collective-permute-done((f32[128,4]{1,0:T(8,128)S(1)}, f32[128,4]{1,0:T(8,128)S(1)}, u32[]{:S(2)}, u32[]{:S(2)}) %collective-permute-start.4) | collective-permute-done | bytes 2080 | tf_op jit(solution)/shard_map/ppermute | solution.py:295
  46.2 0.0 copy-done.4
  46.2 0.2 shard_map.63.weights_ref
  46.4 3.7 %collective-permute-done.5.refs_0_ = bf16[384,512]{1,0:T(8,128)(2,1)S(1)} collective-permute-done((bf16[384,512]{1,0:T(8,128)(2,1)S(1)}, bf16[384,512]{1,0:T(8,128)(2,1)S(1)}, u32[]{:S(2)}, u32[]{:S(2)}) %collective-permute-start.5) | collective-permute-done | bytes 393248 | tf_op jit(solution)/shard_map/ppermute | solution.py:244
  50.1 2.2 %collective-permute-done.6.refs_1_ = bf16[384,512]{1,0:T(8,128)(2,1)S(1)} collective-permute-done((bf16[384,512]{1,0:T(8,128)(2,1)S(1)}, bf16[384,512]{1,0:T(8,128)(2,1)S(1)}, u32[]{:S(2)}, u32[]{:S(2)}) %collective-permute-start.6) | collective-permute-done | bytes 393248 | tf_op jit(solution)/shard_map/ppermute | solution.py:244
  52.3 0.3 collective-permute-done.7.refs_2_
  52.6 0.4 shard_map.64
  53.0 17.5 %all_to_all.11.arrived_ref = bf16[64,8,512]{2,1,0:T(8,128)(2,1)S(1)} all-to-all(bf16[64,8,512]{2,1,0:T(8,128)(2,1)S(1)} %bitcast.18), channel_id=1, replica_groups=mesh['expert'=4,'row'=16,'col'=2] {'expert','row'}, dimensions={0} | all-to-all | bytes 1048576 | tf_op jit(solution)/shard_map/all_to_all | solution.py:305
  70.6 1.0 %shard_map.65 = bf16[128,2048]{1,0:T(8,128)(2,1)} custom-call(s32[1]{0:T(128)} %bitcast.core_ref, bf16[64,8,512]{2,1,0:T(8,128)(2,1)S(1)} %all_to_all.11.arrived_ref, bf16[128,64]{1,0:T(8,128)(2,1)S(1)} %shard_map.63.weights_ref), custom_call_target="tpu_custom_call" | custom-call | tf_op jit(solution)/shard_map/pallas_call | solution.py:208
Async XLA Ops:
  0.0 1.1 %copy-start = (bf16[128,2048]{1,0:T(8,128)(2,1)S(1)}, bf16[128,2048]{1,0:T(8,128)(2,1)}, u32[]{:S(2)}) copy-start(bf16[128,2048]{1,0:T(8,128)(2,1)} %param.5) | copy-start | bytes 1572868
  26.4 9.1 %collective-permute-start = (bf16[384,512]{1,0:T(8,128)(2,1)S(1)}, bf16[384,512]{1,0:T(8,128)(2,1)S(1)}, u32[]{:S(2)}, u32[]{:S(2)}) collective-permute-start(bf16[384,512]{1,0:T(8,128)(2,1)S(1)} %get-tuple-element.19.rows_ref), channel_id=1, source_target_pairs={{0,6},{1,3},{2,4},{3,1},{4,2},{5,7},{6,0},{7,5},{8,14},{9,11},{10,... | collective-permute-start | bytes 1179656 | tf_op jit(solution)/shard_map/ppermute | solution.py:244
  27.4 8.6 %collective-permute-start.1 = (bf16[384,512]{1,0:T(8,128)(2,1)S(1)}, bf16[384,512]{1,0:T(8,128)(2,1)S(1)}, u32[]{:S(2)}, u32[]{:S(2)}) collective-permute-start(bf16[384,512]{1,0:T(8,128)(2,1)S(1)} %get-tuple-element.19.rows_ref), channel_id=1, source_target_pairs={{0,2},{1,9},{2,0},{3,11},{4,6},{5,13},{6,4},{7,15},{8,10},{9,1},{1... | collective-permute-start | bytes 1179656 | tf_op jit(solution)/shard_map/ppermute | solution.py:244
  27.8 8.9 %collective-permute-start.2 = (bf16[384,512]{1,0:T(8,128)(2,1)S(1)}, bf16[384,512]{1,0:T(8,128)(2,1)S(1)}, u32[]{:S(2)}, u32[]{:S(2)}) collective-permute-start(bf16[384,512]{1,0:T(8,128)(2,1)S(1)} %get-tuple-element.19.rows_ref), channel_id=1, source_target_pairs={{0,8},{1,25},{2,10},{3,27},{4,12},{5,29},{6,14},{7,31},{8,0},{9,17... | collective-permute-start | bytes 1179656 | tf_op jit(solution)/shard_map/ppermute | solution.py:244
  27.8 2.0 %copy-start.1 = (bf16[1,2048,896]{2,1,0:T(8,128)(2,1)S(1)}, bf16[1,2048,896]{2,1,0:T(8,128)(2,1)}, u32[]{:S(2)}) copy-start(bf16[1,2048,896]{2,1,0:T(8,128)(2,1)} %param.7) | copy-start | bytes 11010052
  29.8 5.6 %copy-start.2 = (bf16[1,2048,896]{2,1,0:T(8,128)(2,1)S(1)}, bf16[1,2048,896]{2,1,0:T(8,128)(2,1)}, u32[]{:S(2)}) copy-start(bf16[1,2048,896]{2,1,0:T(8,128)(2,1)} %param.7) | copy-start | bytes 11010052
  36.6 2.8 %copy-start.3 = (bf16[1,896,2048]{2,1,0:T(8,128)(2,1)S(1)}, bf16[1,896,2048]{2,1,0:T(8,128)(2,1)}, u32[]{:S(2)}) copy-start(bf16[1,896,2048]{2,1,0:T(8,128)(2,1)} %param.8) | copy-start | bytes 11010052
  37.2 2.2 %collective-permute-start.3 = (bf16[384,896]{1,0:T(8,128)(2,1)S(1)}, bf16[384,896]{1,0:T(8,128)(2,1)S(1)}, u32[]{:S(2)}, u32[]{:S(2)}) collective-permute-start(bf16[384,896]{1,0:T(8,128)(2,1)S(1)} %get-tuple-element.21), channel_id=1, source_target_pairs={{0,1},{1,0},{2,3},{3,2},{4,5},{5,4},{6,7},{7,6},{8,9},{9,8},{10,11... | collective-permute-start | bytes 2064392 | tf_op jit(solution)/shard_map/ppermute | solution.py:271
  41.0 9.1 %collective-permute-start.5 = (bf16[384,512]{1,0:T(8,128)(2,1)S(1)}, bf16[384,512]{1,0:T(8,128)(2,1)S(1)}, u32[]{:S(2)}, u32[]{:S(2)}) collective-permute-start(bf16[384,512]{1,0:T(8,128)(2,1)S(1)} %get-tuple-element.28), channel_id=1, source_target_pairs={{0,6},{1,3},{2,4},{3,1},{4,2},{5,7},{6,0},{7,5},{8,14},{9,11},{10,... | collective-permute-start | bytes 1179656 | tf_op jit(solution)/shard_map/ppermute | solution.py:244
  42.5 9.7 %collective-permute-start.6 = (bf16[384,512]{1,0:T(8,128)(2,1)S(1)}, bf16[384,512]{1,0:T(8,128)(2,1)S(1)}, u32[]{:S(2)}, u32[]{:S(2)}) collective-permute-start(bf16[384,512]{1,0:T(8,128)(2,1)S(1)} %get-tuple-element.29), channel_id=1, source_target_pairs={{0,2},{1,9},{2,0},{3,11},{4,6},{5,13},{6,4},{7,15},{8,10},{9,1},{1... | collective-permute-start | bytes 1179656 | tf_op jit(solution)/shard_map/ppermute | solution.py:244
  43.4 9.2 %collective-permute-start.7 = (bf16[384,512]{1,0:T(8,128)(2,1)S(1)}, bf16[384,512]{1,0:T(8,128)(2,1)S(1)}, u32[]{:S(2)}, u32[]{:S(2)}) collective-permute-start(bf16[384,512]{1,0:T(8,128)(2,1)S(1)} %get-tuple-element.30), channel_id=1, source_target_pairs={{0,8},{1,25},{2,10},{3,27},{4,12},{5,29},{6,14},{7,31},{8,0},{9,17... | collective-permute-start | bytes 1179656 | tf_op jit(solution)/shard_map/ppermute | solution.py:244
  43.9 0.7 %copy-start.5 = (bf16[2048,4]{0,1:T(4,128)(2,1)S(1)}, bf16[2048,4]{0,1:T(4,128)(2,1)}, u32[]{:S(2)}) copy-start(bf16[2048,4]{0,1:T(4,128)(2,1)} %param.6) | copy-start | bytes 49156
  43.9 2.3 %copy-start.4 = (s32[1,4,8]{2,1,0:T(4,128)S(1)}, s32[1,4,8]{2,1,0:T(4,128)}, u32[]{:S(2)}) copy-start(s32[1,4,8]{2,1,0:T(4,128)} %choices_ref.1) | copy-start | bytes 388
  44.9 1.3 %collective-permute-start.4 = (f32[128,4]{1,0:T(8,128)S(1)}, f32[128,4]{1,0:T(8,128)S(1)}, u32[]{:S(2)}, u32[]{:S(2)}) collective-permute-start(f32[128,4]{1,0:T(8,128)S(1)} %convolution_bitcast_fusion.logits_ref), channel_id=1, source_target_pairs={{0,1},{1,0},{2,3},{3,2},{4,5},{5,4},{6,7},{7,6},{8,9},{9,8},{10,11... | collective-permute-start | bytes 6152 | tf_op jit(solution)/shard_map/ppermute | solution.py:295
where the time goes:
time: 71.8 us; the launch traced here: 71.6 us
  blocking collectives  41.9 us (58%)
  waiting for transfers between devices  14.6 us (20%)
  Pallas kernels  6.77 us (9%)
  starting transfers between devices  4.38 us (6%)
  local copies, waits for them, and re-layouts  3.17 us (4%)
    all_to_all x1, blocking collectives, on_device(): lax.all_to_all(spread, ('expert', 'row'), split_axis=0, concat_axis=0, ti...  24.4 us
    all_to_all x1, blocking collectives, on_device(): lax.all_to_all(out.reshape(sources, slots, quarter), ('expert', 'row'), s...  17.5 us
    ppermute x6, waiting for transfers between devices, send(): return lax.ppermute(array, ('row', 'col'), pairs_of(move))  11.2 us
    pallas_call x11, Pallas kernels, call(): pl.pallas_call(kernel, out_shape=outs, in_specs=[pl.BlockSpec(memory_spac...  6.77 us
    ppermute x6, starting transfers between devices, send(): return lax.ppermute(array, ('row', 'col'), pairs_of(move))  4.21 us
    unnamed x12, local copies, waits for them, and re-layouts  2.35 us
    ppermute x1, waiting for transfers between devices, on_device(): other = lax.ppermute(rounded, 'col', swap)  2.13 us
  transfers between devices with their start and end apart: 8, of which 6 were waited for; matrix products, arithmetic and copies ran while one was open for 0% of the time, Pallas kernels for 4%

commit v1 on v0

--- a/solution.py
+++ b/solution.py
@@ -76,15 +76,19 @@
 def compact_kernel(x_ref, full_ref, where_ref):
     rows = x_ref.shape[0]
     capacity = full_ref.shape[0]
-    live = (x_ref[:, :128].astype(jnp.float32) < EMPTY - 1.0).astype(jnp.bfloat16)
-    i = lax.broadcasted_iota(jnp.int32, (rows, rows), 0)
-    j = lax.broadcasted_iota(jnp.int32, (rows, rows), 1)
-    contract = (((0,), (0,)), ((), ()))
-    upto = lax.dot_general(
-        live, (i <= j).astype(jnp.bfloat16), contract, preferred_element_type=jnp.float32
-    )[:8]
-    before = jnp.where(j[:8] == 0, 0.0, pltpu.roll(upto, 1, 1))
-    position = jnp.where(upto > before, before, -1.0).astype(jnp.int32)[:1]
+    live = (x_ref[:, :128].astype(jnp.float32) < EMPTY - 1.0).astype(jnp.float32)
+    i = lax.broadcasted_iota(jnp.int32, (BAND, BAND), 0)
+    j = lax.broadcasted_iota(jnp.int32, (BAND, BAND), 1)
+    masks = jnp.concatenate([(i < j).astype(jnp.bfloat16), (i == j).astype(jnp.bfloat16)], axis=1)
+    offset, position = 0.0, []
+    for row in range(0, rows, BAND):
+        part = live[row : row + BAND]
+        both = lax.dot_general(
+            part.astype(jnp.bfloat16), masks, (((0,), (0,)), ((), ())), preferred_element_type=jnp.float32
+        )[:8]
+        position.append(jnp.where(both[:, BAND:] > 0.5, both[:, :BAND] + offset, -1.0))
+        offset += jnp.sum(part, axis=0, keepdims=True)
+    position = jnp.concatenate(position, axis=1).astype(jnp.int32)[:1]
     for p in range(0, capacity, BAND):
         columns = slice(p, p + 2 * BAND)
         target = lax.broadcasted_iota(jnp.int32, (BAND, 2 * BAND), 0) + p

time: 71.8 us -> 71.7 us (level)
  no operation moved by 1% of the time
where the time goes in v1:
time: 71.7 us; the launch traced here: 71.5 us
  blocking collectives  41.9 us (58%)
  waiting for transfers between devices  14.6 us (20%)
  Pallas kernels  6.65 us (9%)
  starting transfers between devices  4.39 us (6%)
  local copies, waits for them, and re-layouts  3.17 us (4%)
    all_to_all x1, blocking collectives, on_device(): lax.all_to_all(spread, ('expert', 'row'), split_axis=0, concat_axis=0, ti...  24.4 us
    all_to_all x1, blocking collectives, on_device(): lax.all_to_all(out.reshape(sources, slots, quarter), ('expert', 'row'), s...  17.5 us
    ppermute x6, waiting for transfers between devices, send(): return lax.ppermute(array, ('row', 'col'), pairs_of(move))  11.2 us
    pallas_call x11, Pallas kernels, call(): pl.pallas_call(kernel, out_shape=outs, in_specs=[pl.BlockSpec(memory_spac...  6.65 us
    ppermute x6, starting transfers between devices, send(): return lax.ppermute(array, ('row', 'col'), pairs_of(move))  4.22 us
    unnamed x12, local copies, waits for them, and re-layouts  2.35 us
    ppermute x1, waiting for transfers between devices, on_device(): other = lax.ppermute(rounded, 'col', swap)  2.13 us
  transfers between devices with their start and end apart: 8, of which 6 were waited for; matrix products, arithmetic and copies ran while one was open for 0% of the time, Pallas kernels for 4%

profile of v1, /device:TPU:0, one launch (start us, length us, event | category | flops | bytes accessed | tf_op | source)
XLA Modules:
  0.0 71.5 jit_solution(5546973107466863918)
XLA Ops:
  0.0 0.0 copy-start
  0.0 0.8 %eq.24 = s32[32]{0:T(128)S(1)} reshape(s32[1,4,8]{2,1,0:T(4,128)} %choices_ref.1) | data formatting | bytes 256 | tf_op jit(solution)/shard_map/eq | solution.py:251
  0.8 0.1 fusion.hot_ref
  0.9 0.2 copy-done
  1.1 0.2 fusion.1.picked_ref
  1.3 0.1 shard_map.55
  1.4 24.4 %all_to_all.10 = bf16[64,8,512]{2,1,0:T(8,128)(2,1)S(1)} all-to-all(bf16[64,8,512]{2,1,0:T(8,128)(2,1)S(1)} %shard_map.55), channel_id=1, replica_groups=mesh['expert'=4,'row'=16,'col'=2] {'expert','row'}, dimensions={0} | all-to-all | bytes 1048576 | tf_op jit(solution)/shard_map/all_to_all | solution.py:255
  25.8 0.4 shard_map.56
  26.3 1.1 %collective-permute-start = (bf16[384,512]{1,0:T(8,128)(2,1)S(1)}, bf16[384,512]{1,0:T(8,128)(2,1)S(1)}, u32[]{:S(2)}, u32[]{:S(2)}) collective-permute-start(bf16[384,512]{1,0:T(8,128)(2,1)S(1)} %get-tuple-element.19.rows_ref), channel_id=1, source_target_pairs={{0,6},{1,3},{2,4},{3,1},{4,2},{5,7},{6,0},{7,5},{8,14},{9,11},{10,... | collective-permute-start | bytes 1179656 | tf_op jit(solution)/shard_map/ppermute | solution.py:248
  27.3 0.3 collective-permute-start.1
  27.7 0.0 collective-permute-start.2
  27.7 0.0 copy-start.1
  27.7 2.0 %copy-done.1 = bf16[1,2048,896]{2,1,0:T(8,128)(2,1)S(1)} copy-done((bf16[1,2048,896]{2,1,0:T(8,128)(2,1)S(1)}, bf16[1,2048,896]{2,1,0:T(8,128)(2,1)}, u32[]{:S(2)}) %copy-start.1) | copy-done | bytes 3670040
  29.7 0.0 copy-start.2
  29.7 0.6 shard_map.57.sum_ref
  30.3 5.1 %collective-permute-done.rows_ref = bf16[384,512]{1,0:T(8,128)(2,1)S(1)} collective-permute-done((bf16[384,512]{1,0:T(8,128)(2,1)S(1)}, bf16[384,512]{1,0:T(8,128)(2,1)S(1)}, u32[]{:S(2)}, u32[]{:S(2)}) %collective-permute-start) | collective-permute-done | bytes 393248 | tf_op jit(solution)/shard_map/ppermute | solution.py:248
  35.3 0.0 copy-done.2
  35.3 0.6 shard_map.58.sum_ref
  35.9 0.0 collective-permute-done.1.rows_ref
  35.9 0.6 shard_map.59.sum_ref
  36.5 0.0 copy-start.3
  36.5 0.0 collective-permute-done.2.rows_ref
  36.5 0.6 shard_map.60
  37.1 0.1 collective-permute-start.3
  37.2 2.1 %collective-permute-done.3.other_ref = bf16[384,896]{1,0:T(8,128)(2,1)S(1)} collective-permute-done((bf16[384,896]{1,0:T(8,128)(2,1)S(1)}, bf16[384,896]{1,0:T(8,128)(2,1)S(1)}, u32[]{:S(2)}, u32[]{:S(2)}) %collective-permute-start.3) | collective-permute-done | bytes 688160 | tf_op jit(solution)/shard_map/ppermute | solution.py:275
  39.3 0.0 copy-done.3
  39.4 1.6 %shard_map.61 = (bf16[384,896]{1,0:T(8,128)(2,1)S(1)}, bf16[384,512]{1,0:T(8,128)(2,1)S(1)}, bf16[384,512]{1,0:T(8,128)(2,1)S(1)}, bf16[384,512]{1,0:T(8,128)(2,1)S(1)}) custom-call(s32[1]{0:T(128)} %bitcast.1.mine_ref, s32[1]{0:T(128)} %bitcast.core_ref, f32[384,896]{1,0:T(8,128)S(1)} %get-tuple-element.20.sum_ref, ...), custom_call_target="tpu_custom_call" | custom-call | tf_op jit(solution)/shard_map/pallas_call | solution.py:212
  40.9 1.5 %collective-permute-start.5 = (bf16[384,512]{1,0:T(8,128)(2,1)S(1)}, bf16[384,512]{1,0:T(8,128)(2,1)S(1)}, u32[]{:S(2)}, u32[]{:S(2)}) collective-permute-start(bf16[384,512]{1,0:T(8,128)(2,1)S(1)} %get-tuple-element.28), channel_id=1, source_target_pairs={{0,6},{1,3},{2,4},{3,1},{4,2},{5,7},{6,0},{7,5},{8,14},{9,11},{10,... | collective-permute-start | bytes 1179656 | tf_op jit(solution)/shard_map/ppermute | solution.py:248
  42.4 0.8 %collective-permute-start.6 = (bf16[384,512]{1,0:T(8,128)(2,1)S(1)}, bf16[384,512]{1,0:T(8,128)(2,1)S(1)}, u32[]{:S(2)}, u32[]{:S(2)}) collective-permute-start(bf16[384,512]{1,0:T(8,128)(2,1)S(1)} %get-tuple-element.29), channel_id=1, source_target_pairs={{0,2},{1,9},{2,0},{3,11},{4,6},{5,13},{6,4},{7,15},{8,10},{9,1},{1... | collective-permute-start | bytes 1179656 | tf_op jit(solution)/shard_map/ppermute | solution.py:248
  43.3 0.5 collective-permute-start.7
  43.8 0.0 copy-start.5
  43.8 0.0 copy-start.4
  43.8 0.6 shard_map.62
  44.3 0.1 copy-done.5
  44.5 0.3 convolution_bitcast_fusion.logits_ref
  44.7 0.1 collective-permute-start.4
  44.8 1.2 %collective-permute-done.4.other_ref = f32[128,4]{1,0:T(8,128)S(1)} collective-permute-done((f32[128,4]{1,0:T(8,128)S(1)}, f32[128,4]{1,0:T(8,128)S(1)}, u32[]{:S(2)}, u32[]{:S(2)}) %collective-permute-start.4) | collective-permute-done | bytes 2080 | tf_op jit(solution)/shard_map/ppermute | solution.py:299
  46.1 0.0 copy-done.4
  46.1 0.2 shard_map.63.weights_ref
  46.3 3.7 %collective-permute-done.5.refs_0_ = bf16[384,512]{1,0:T(8,128)(2,1)S(1)} collective-permute-done((bf16[384,512]{1,0:T(8,128)(2,1)S(1)}, bf16[384,512]{1,0:T(8,128)(2,1)S(1)}, u32[]{:S(2)}, u32[]{:S(2)}) %collective-permute-start.5) | collective-permute-done | bytes 393248 | tf_op jit(solution)/shard_map/ppermute | solution.py:248
  50.0 2.2 %collective-permute-done.6.refs_1_ = bf16[384,512]{1,0:T(8,128)(2,1)S(1)} collective-permute-done((bf16[384,512]{1,0:T(8,128)(2,1)S(1)}, bf16[384,512]{1,0:T(8,128)(2,1)S(1)}, u32[]{:S(2)}, u32[]{:S(2)}) %collective-permute-start.6) | collective-permute-done | bytes 393248 | tf_op jit(solution)/shard_map/ppermute | solution.py:248
  52.2 0.3 collective-permute-done.7.refs_2_
  52.5 0.4 shard_map.64
  52.9 17.5 %all_to_all.11.arrived_ref = bf16[64,8,512]{2,1,0:T(8,128)(2,1)S(1)} all-to-all(bf16[64,8,512]{2,1,0:T(8,128)(2,1)S(1)} %bitcast.18), channel_id=1, replica_groups=mesh['expert'=4,'row'=16,'col'=2] {'expert','row'}, dimensions={0} | all-to-all | bytes 1048576 | tf_op jit(solution)/shard_map/all_to_all | solution.py:309
  70.4 1.0 %shard_map.65 = bf16[128,2048]{1,0:T(8,128)(2,1)} custom-call(s32[1]{0:T(128)} %bitcast.core_ref, bf16[64,8,512]{2,1,0:T(8,128)(2,1)S(1)} %all_to_all.11.arrived_ref, bf16[128,64]{1,0:T(8,128)(2,1)S(1)} %shard_map.63.weights_ref), custom_call_target="tpu_custom_call" | custom-call | tf_op jit(solution)/shard_map/pallas_call | solution.py:212
Async XLA Ops:
  0.0 1.1 %copy-start = (bf16[128,2048]{1,0:T(8,128)(2,1)S(1)}, bf16[128,2048]{1,0:T(8,128)(2,1)}, u32[]{:S(2)}) copy-start(bf16[128,2048]{1,0:T(8,128)(2,1)} %param.5) | copy-start | bytes 1572868
  26.3 9.1 %collective-permute-start = (bf16[384,512]{1,0:T(8,128)(2,1)S(1)}, bf16[384,512]{1,0:T(8,128)(2,1)S(1)}, u32[]{:S(2)}, u32[]{:S(2)}) collective-permute-start(bf16[384,512]{1,0:T(8,128)(2,1)S(1)} %get-tuple-element.19.rows_ref), channel_id=1, source_target_pairs={{0,6},{1,3},{2,4},{3,1},{4,2},{5,7},{6,0},{7,5},{8,14},{9,11},{10,... | collective-permute-start | bytes 1179656 | tf_op jit(solution)/shard_map/ppermute | solution.py:248
  27.3 8.6 %collective-permute-start.1 = (bf16[384,512]{1,0:T(8,128)(2,1)S(1)}, bf16[384,512]{1,0:T(8,128)(2,1)S(1)}, u32[]{:S(2)}, u32[]{:S(2)}) collective-permute-start(bf16[384,512]{1,0:T(8,128)(2,1)S(1)} %get-tuple-element.19.rows_ref), channel_id=1, source_target_pairs={{0,2},{1,9},{2,0},{3,11},{4,6},{5,13},{6,4},{7,15},{8,10},{9,1},{1... | collective-permute-start | bytes 1179656 | tf_op jit(solution)/shard_map/ppermute | solution.py:248
  27.7 8.9 %collective-permute-start.2 = (bf16[384,512]{1,0:T(8,128)(2,1)S(1)}, bf16[384,512]{1,0:T(8,128)(2,1)S(1)}, u32[]{:S(2)}, u32[]{:S(2)}) collective-permute-start(bf16[384,512]{1,0:T(8,128)(2,1)S(1)} %get-tuple-element.19.rows_ref), channel_id=1, source_target_pairs={{0,8},{1,25},{2,10},{3,27},{4,12},{5,29},{6,14},{7,31},{8,0},{9,17... | collective-permute-start | bytes 1179656 | tf_op jit(solution)/shard_map/ppermute | solution.py:248
  27.7 2.0 %copy-start.1 = (bf16[1,2048,896]{2,1,0:T(8,128)(2,1)S(1)}, bf16[1,2048,896]{2,1,0:T(8,128)(2,1)}, u32[]{:S(2)}) copy-start(bf16[1,2048,896]{2,1,0:T(8,128)(2,1)} %param.7) | copy-start | bytes 11010052
  29.7 5.6 %copy-start.2 = (bf16[1,2048,896]{2,1,0:T(8,128)(2,1)S(1)}, bf16[1,2048,896]{2,1,0:T(8,128)(2,1)}, u32[]{:S(2)}) copy-start(bf16[1,2048,896]{2,1,0:T(8,128)(2,1)} %param.7) | copy-start | bytes 11010052
  36.5 2.8 %copy-start.3 = (bf16[1,896,2048]{2,1,0:T(8,128)(2,1)S(1)}, bf16[1,896,2048]{2,1,0:T(8,128)(2,1)}, u32[]{:S(2)}) copy-start(bf16[1,896,2048]{2,1,0:T(8,128)(2,1)} %param.8) | copy-start | bytes 11010052
  37.1 2.2 %collective-permute-start.3 = (bf16[384,896]{1,0:T(8,128)(2,1)S(1)}, bf16[384,896]{1,0:T(8,128)(2,1)S(1)}, u32[]{:S(2)}, u32[]{:S(2)}) collective-permute-start(bf16[384,896]{1,0:T(8,128)(2,1)S(1)} %get-tuple-element.21), channel_id=1, source_target_pairs={{0,1},{1,0},{2,3},{3,2},{4,5},{5,4},{6,7},{7,6},{8,9},{9,8},{10,11... | collective-permute-start | bytes 2064392 | tf_op jit(solution)/shard_map/ppermute | solution.py:275
  40.9 9.1 %collective-permute-start.5 = (bf16[384,512]{1,0:T(8,128)(2,1)S(1)}, bf16[384,512]{1,0:T(8,128)(2,1)S(1)}, u32[]{:S(2)}, u32[]{:S(2)}) collective-permute-start(bf16[384,512]{1,0:T(8,128)(2,1)S(1)} %get-tuple-element.28), channel_id=1, source_target_pairs={{0,6},{1,3},{2,4},{3,1},{4,2},{5,7},{6,0},{7,5},{8,14},{9,11},{10,... | collective-permute-start | bytes 1179656 | tf_op jit(solution)/shard_map/ppermute | solution.py:248
  42.4 9.7 %collective-permute-start.6 = (bf16[384,512]{1,0:T(8,128)(2,1)S(1)}, bf16[384,512]{1,0:T(8,128)(2,1)S(1)}, u32[]{:S(2)}, u32[]{:S(2)}) collective-permute-start(bf16[384,512]{1,0:T(8,128)(2,1)S(1)} %get-tuple-element.29), channel_id=1, source_target_pairs={{0,2},{1,9},{2,0},{3,11},{4,6},{5,13},{6,4},{7,15},{8,10},{9,1},{1... | collective-permute-start | bytes 1179656 | tf_op jit(solution)/shard_map/ppermute | solution.py:248
  43.3 9.2 %collective-permute-start.7 = (bf16[384,512]{1,0:T(8,128)(2,1)S(1)}, bf16[384,512]{1,0:T(8,128)(2,1)S(1)}, u32[]{:S(2)}, u32[]{:S(2)}) collective-permute-start(bf16[384,512]{1,0:T(8,128)(2,1)S(1)} %get-tuple-element.30), channel_id=1, source_target_pairs={{0,8},{1,25},{2,10},{3,27},{4,12},{5,29},{6,14},{7,31},{8,0},{9,17... | collective-permute-start | bytes 1179656 | tf_op jit(solution)/shard_map/ppermute | solution.py:248
  43.8 0.7 %copy-start.5 = (bf16[2048,4]{0,1:T(4,128)(2,1)S(1)}, bf16[2048,4]{0,1:T(4,128)(2,1)}, u32[]{:S(2)}) copy-start(bf16[2048,4]{0,1:T(4,128)(2,1)} %param.6) | copy-start | bytes 49156
  43.8 2.3 %copy-start.4 = (s32[1,4,8]{2,1,0:T(4,128)S(1)}, s32[1,4,8]{2,1,0:T(4,128)}, u32[]{:S(2)}) copy-start(s32[1,4,8]{2,1,0:T(4,128)} %choices_ref.1) | copy-start | bytes 388
  44.7 1.3 %collective-permute-start.4 = (f32[128,4]{1,0:T(8,128)S(1)}, f32[128,4]{1,0:T(8,128)S(1)}, u32[]{:S(2)}, u32[]{:S(2)}) collective-permute-start(f32[128,4]{1,0:T(8,128)S(1)} %convolution_bitcast_fusion.logits_ref), channel_id=1, source_target_pairs={{0,1},{1,0},{2,3},{3,2},{4,5},{5,4},{6,7},{7,6},{8,9},{9,8},{10,11... | collective-permute-start | bytes 6152 | tf_op jit(solution)/shard_map/ppermute | solution.py:299

commit v2 on v1

--- a/solution.py
+++ b/solution.py
@@ -125,8 +125,8 @@
 
 def down_kernel(mine_ref, core_ref, sum_ref, other_ref, down_ref, hidden_ref, *out_refs):
     rows = hidden_ref.shape[0]
-    block = rows // 2
-    for i in range(2):
+    block = rows
+    for i in range(1):
         at = slice(i * block, (i + 1) * block)
         value = sum_ref[at, :] + other_ref[at, :].astype(jnp.float32)
         hidden = jax.nn.gelu(value, approximate=True).astype(jnp.bfloat16)

time: 71.7 us -> 71.8 us (level)
  no operation moved by 1% of the time
where the time goes in v2:
time: 71.8 us; the launch traced here: 71.5 us
  blocking collectives  41.9 us (58%)
  waiting for transfers between devices  14.6 us (20%)
  Pallas kernels  6.66 us (9%)
  starting transfers between devices  4.39 us (6%)
  local copies, waits for them, and re-layouts  3.17 us (4%)
    all_to_all x1, blocking collectives, on_device(): lax.all_to_all(spread, ('expert', 'row'), split_axis=0, concat_axis=0, ti...  24.4 us
    all_to_all x1, blocking collectives, on_device(): lax.all_to_all(out.reshape(sources, slots, quarter), ('expert', 'row'), s...  17.5 us
    ppermute x6, waiting for transfers between devices, send(): return lax.ppermute(array, ('row', 'col'), pairs_of(move))  11.2 us
    pallas_call x11, Pallas kernels, call(): pl.pallas_call(kernel, out_shape=outs, in_specs=[pl.BlockSpec(memory_spac...  6.66 us
    ppermute x6, starting transfers between devices, send(): return lax.ppermute(array, ('row', 'col'), pairs_of(move))  4.22 us
    unnamed x12, local copies, waits for them, and re-layouts  2.35 us
    ppermute x1, waiting for transfers between devices, on_device(): other = lax.ppermute(rounded, 'col', swap)  2.13 us
  transfers between devices with their start and end apart: 8, of which 6 were waited for; matrix products, arithmetic and copies ran while one was open for 0% of the time, Pallas kernels for 4%

profile of v2, /device:TPU:0, one launch (start us, length us, event | category | flops | bytes accessed | tf_op | source)
XLA Modules:
  0.0 71.5 jit_solution(14194480701342558074)
XLA Ops:
  0.0 0.0 copy-start
  0.0 0.8 %eq.24 = s32[32]{0:T(128)S(1)} reshape(s32[1,4,8]{2,1,0:T(4,128)} %choices_ref.1) | data formatting | bytes 256 | tf_op jit(solution)/shard_map/eq | solution.py:251
  0.8 0.1 fusion.hot_ref
  0.9 0.2 copy-done
  1.1 0.2 fusion.1.picked_ref
  1.3 0.1 shard_map.55
  1.4 24.4 %all_to_all.10 = bf16[64,8,512]{2,1,0:T(8,128)(2,1)S(1)} all-to-all(bf16[64,8,512]{2,1,0:T(8,128)(2,1)S(1)} %shard_map.55), channel_id=1, replica_groups=mesh['expert'=4,'row'=16,'col'=2] {'expert','row'}, dimensions={0} | all-to-all | bytes 1048576 | tf_op jit(solution)/shard_map/all_to_all | solution.py:255
  25.8 0.4 shard_map.56
  26.3 1.1 %collective-permute-start = (bf16[384,512]{1,0:T(8,128)(2,1)S(1)}, bf16[384,512]{1,0:T(8,128)(2,1)S(1)}, u32[]{:S(2)}, u32[]{:S(2)}) collective-permute-start(bf16[384,512]{1,0:T(8,128)(2,1)S(1)} %get-tuple-element.19.rows_ref), channel_id=1, source_target_pairs={{0,6},{1,3},{2,4},{3,1},{4,2},{5,7},{6,0},{7,5},{8,14},{9,11},{10,... | collective-permute-start | bytes 1179656 | tf_op jit(solution)/shard_map/ppermute | solution.py:248
  27.3 0.3 collective-permute-start.1
  27.7 0.0 collective-permute-start.2
  27.7 0.0 copy-start.1
  27.7 2.0 %copy-done.1 = bf16[1,2048,896]{2,1,0:T(8,128)(2,1)S(1)} copy-done((bf16[1,2048,896]{2,1,0:T(8,128)(2,1)S(1)}, bf16[1,2048,896]{2,1,0:T(8,128)(2,1)}, u32[]{:S(2)}) %copy-start.1) | copy-done | bytes 3670040
  29.7 0.0 copy-start.2
  29.7 0.6 shard_map.57.sum_ref
  30.3 5.1 %collective-permute-done.rows_ref = bf16[384,512]{1,0:T(8,128)(2,1)S(1)} collective-permute-done((bf16[384,512]{1,0:T(8,128)(2,1)S(1)}, bf16[384,512]{1,0:T(8,128)(2,1)S(1)}, u32[]{:S(2)}, u32[]{:S(2)}) %collective-permute-start) | collective-permute-done | bytes 393248 | tf_op jit(solution)/shard_map/ppermute | solution.py:248
  35.3 0.0 copy-done.2
  35.3 0.6 shard_map.58.sum_ref
  35.9 0.0 collective-permute-done.1.rows_ref
  35.9 0.6 shard_map.59.sum_ref
  36.5 0.0 copy-start.3
  36.5 0.0 collective-permute-done.2.rows_ref
  36.5 0.6 shard_map.60
  37.1 0.1 collective-permute-start.3
  37.2 2.1 %collective-permute-done.3.other_ref = bf16[384,896]{1,0:T(8,128)(2,1)S(1)} collective-permute-done((bf16[384,896]{1,0:T(8,128)(2,1)S(1)}, bf16[384,896]{1,0:T(8,128)(2,1)S(1)}, u32[]{:S(2)}, u32[]{:S(2)}) %collective-permute-start.3) | collective-permute-done | bytes 688160 | tf_op jit(solution)/shard_map/ppermute | solution.py:275
  39.3 0.0 copy-done.3
  39.4 1.6 %shard_map.61 = (bf16[384,896]{1,0:T(8,128)(2,1)S(1)}, bf16[384,512]{1,0:T(8,128)(2,1)S(1)}, bf16[384,512]{1,0:T(8,128)(2,1)S(1)}, bf16[384,512]{1,0:T(8,128)(2,1)S(1)}) custom-call(s32[1]{0:T(128)} %bitcast.1.mine_ref, s32[1]{0:T(128)} %bitcast.core_ref, f32[384,896]{1,0:T(8,128)S(1)} %get-tuple-element.20.sum_ref, ...), custom_call_target="tpu_custom_call" | custom-call | tf_op jit(solution)/shard_map/pallas_call | solution.py:212
  40.9 1.5 %collective-permute-start.5 = (bf16[384,512]{1,0:T(8,128)(2,1)S(1)}, bf16[384,512]{1,0:T(8,128)(2,1)S(1)}, u32[]{:S(2)}, u32[]{:S(2)}) collective-permute-start(bf16[384,512]{1,0:T(8,128)(2,1)S(1)} %get-tuple-element.28), channel_id=1, source_target_pairs={{0,6},{1,3},{2,4},{3,1},{4,2},{5,7},{6,0},{7,5},{8,14},{9,11},{10,... | collective-permute-start | bytes 1179656 | tf_op jit(solution)/shard_map/ppermute | solution.py:248
  42.4 0.8 %collective-permute-start.6 = (bf16[384,512]{1,0:T(8,128)(2,1)S(1)}, bf16[384,512]{1,0:T(8,128)(2,1)S(1)}, u32[]{:S(2)}, u32[]{:S(2)}) collective-permute-start(bf16[384,512]{1,0:T(8,128)(2,1)S(1)} %get-tuple-element.29), channel_id=1, source_target_pairs={{0,2},{1,9},{2,0},{3,11},{4,6},{5,13},{6,4},{7,15},{8,10},{9,1},{1... | collective-permute-start | bytes 1179656 | tf_op jit(solution)/shard_map/ppermute | solution.py:248
  43.3 0.5 collective-permute-start.7
  43.8 0.0 copy-start.5
  43.8 0.0 copy-start.4
  43.8 0.6 shard_map.62
  44.3 0.1 copy-done.5
  44.5 0.3 convolution_bitcast_fusion.logits_ref
  44.8 0.1 collective-permute-start.4
  44.9 1.2 %collective-permute-done.4.other_ref = f32[128,4]{1,0:T(8,128)S(1)} collective-permute-done((f32[128,4]{1,0:T(8,128)S(1)}, f32[128,4]{1,0:T(8,128)S(1)}, u32[]{:S(2)}, u32[]{:S(2)}) %collective-permute-start.4) | collective-permute-done | bytes 2080 | tf_op jit(solution)/shard_map/ppermute | solution.py:299
  46.1 0.0 copy-done.4
  46.1 0.2 shard_map.63.weights_ref
  46.3 3.7 %collective-permute-done.5.refs_0_ = bf16[384,512]{1,0:T(8,128)(2,1)S(1)} collective-permute-done((bf16[384,512]{1,0:T(8,128)(2,1)S(1)}, bf16[384,512]{1,0:T(8,128)(2,1)S(1)}, u32[]{:S(2)}, u32[]{:S(2)}) %collective-permute-start.5) | collective-permute-done | bytes 393248 | tf_op jit(solution)/shard_map/ppermute | solution.py:248
  50.0 2.2 %collective-permute-done.6.refs_1_ = bf16[384,512]{1,0:T(8,128)(2,1)S(1)} collective-permute-done((bf16[384,512]{1,0:T(8,128)(2,1)S(1)}, bf16[384,512]{1,0:T(8,128)(2,1)S(1)}, u32[]{:S(2)}, u32[]{:S(2)}) %collective-permute-start.6) | collective-permute-done | bytes 393248 | tf_op jit(solution)/shard_map/ppermute | solution.py:248
  52.2 0.3 collective-permute-done.7.refs_2_
  52.5 0.4 shard_map.64
  52.9 17.5 %all_to_all.11.arrived_ref = bf16[64,8,512]{2,1,0:T(8,128)(2,1)S(1)} all-to-all(bf16[64,8,512]{2,1,0:T(8,128)(2,1)S(1)} %bitcast.18), channel_id=1, replica_groups=mesh['expert'=4,'row'=16,'col'=2] {'expert','row'}, dimensions={0} | all-to-all | bytes 1048576 | tf_op jit(solution)/shard_map/all_to_all | solution.py:309
  70.5 1.0 %shard_map.65 = bf16[128,2048]{1,0:T(8,128)(2,1)} custom-call(s32[1]{0:T(128)} %bitcast.core_ref, bf16[64,8,512]{2,1,0:T(8,128)(2,1)S(1)} %all_to_all.11.arrived_ref, bf16[128,64]{1,0:T(8,128)(2,1)S(1)} %shard_map.63.weights_ref), custom_call_target="tpu_custom_call" | custom-call | tf_op jit(solution)/shard_map/pallas_call | solution.py:212
Async XLA Ops:
  0.0 1.1 %copy-start = (bf16[128,2048]{1,0:T(8,128)(2,1)S(1)}, bf16[128,2048]{1,0:T(8,128)(2,1)}, u32[]{:S(2)}) copy-start(bf16[128,2048]{1,0:T(8,128)(2,1)} %param.5) | copy-start | bytes 1572868
  26.3 9.1 %collective-permute-start = (bf16[384,512]{1,0:T(8,128)(2,1)S(1)}, bf16[384,512]{1,0:T(8,128)(2,1)S(1)}, u32[]{:S(2)}, u32[]{:S(2)}) collective-permute-start(bf16[384,512]{1,0:T(8,128)(2,1)S(1)} %get-tuple-element.19.rows_ref), channel_id=1, source_target_pairs={{0,6},{1,3},{2,4},{3,1},{4,2},{5,7},{6,0},{7,5},{8,14},{9,11},{10,... | collective-permute-start | bytes 1179656 | tf_op jit(solution)/shard_map/ppermute | solution.py:248
  27.3 8.6 %collective-permute-start.1 = (bf16[384,512]{1,0:T(8,128)(2,1)S(1)}, bf16[384,512]{1,0:T(8,128)(2,1)S(1)}, u32[]{:S(2)}, u32[]{:S(2)}) collective-permute-start(bf16[384,512]{1,0:T(8,128)(2,1)S(1)} %get-tuple-element.19.rows_ref), channel_id=1, source_target_pairs={{0,2},{1,9},{2,0},{3,11},{4,6},{5,13},{6,4},{7,15},{8,10},{9,1},{1... | collective-permute-start | bytes 1179656 | tf_op jit(solution)/shard_map/ppermute | solution.py:248
  27.7 8.9 %collective-permute-start.2 = (bf16[384,512]{1,0:T(8,128)(2,1)S(1)}, bf16[384,512]{1,0:T(8,128)(2,1)S(1)}, u32[]{:S(2)}, u32[]{:S(2)}) collective-permute-start(bf16[384,512]{1,0:T(8,128)(2,1)S(1)} %get-tuple-element.19.rows_ref), channel_id=1, source_target_pairs={{0,8},{1,25},{2,10},{3,27},{4,12},{5,29},{6,14},{7,31},{8,0},{9,17... | collective-permute-start | bytes 1179656 | tf_op jit(solution)/shard_map/ppermute | solution.py:248
  27.7 2.0 %copy-start.1 = (bf16[1,2048,896]{2,1,0:T(8,128)(2,1)S(1)}, bf16[1,2048,896]{2,1,0:T(8,128)(2,1)}, u32[]{:S(2)}) copy-start(bf16[1,2048,896]{2,1,0:T(8,128)(2,1)} %param.7) | copy-start | bytes 11010052
  29.7 5.6 %copy-start.2 = (bf16[1,2048,896]{2,1,0:T(8,128)(2,1)S(1)}, bf16[1,2048,896]{2,1,0:T(8,128)(2,1)}, u32[]{:S(2)}) copy-start(bf16[1,2048,896]{2,1,0:T(8,128)(2,1)} %param.7) | copy-start | bytes 11010052
  36.5 2.8 %copy-start.3 = (bf16[1,896,2048]{2,1,0:T(8,128)(2,1)S(1)}, bf16[1,896,2048]{2,1,0:T(8,128)(2,1)}, u32[]{:S(2)}) copy-start(bf16[1,896,2048]{2,1,0:T(8,128)(2,1)} %param.8) | copy-start | bytes 11010052
  37.1 2.2 %collective-permute-start.3 = (bf16[384,896]{1,0:T(8,128)(2,1)S(1)}, bf16[384,896]{1,0:T(8,128)(2,1)S(1)}, u32[]{:S(2)}, u32[]{:S(2)}) collective-permute-start(bf16[384,896]{1,0:T(8,128)(2,1)S(1)} %get-tuple-element.21), channel_id=1, source_target_pairs={{0,1},{1,0},{2,3},{3,2},{4,5},{5,4},{6,7},{7,6},{8,9},{9,8},{10,11... | collective-permute-start | bytes 2064392 | tf_op jit(solution)/shard_map/ppermute | solution.py:275
  40.9 9.1 %collective-permute-start.5 = (bf16[384,512]{1,0:T(8,128)(2,1)S(1)}, bf16[384,512]{1,0:T(8,128)(2,1)S(1)}, u32[]{:S(2)}, u32[]{:S(2)}) collective-permute-start(bf16[384,512]{1,0:T(8,128)(2,1)S(1)} %get-tuple-element.28), channel_id=1, source_target_pairs={{0,6},{1,3},{2,4},{3,1},{4,2},{5,7},{6,0},{7,5},{8,14},{9,11},{10,... | collective-permute-start | bytes 1179656 | tf_op jit(solution)/shard_map/ppermute | solution.py:248
  42.4 9.7 %collective-permute-start.6 = (bf16[384,512]{1,0:T(8,128)(2,1)S(1)}, bf16[384,512]{1,0:T(8,128)(2,1)S(1)}, u32[]{:S(2)}, u32[]{:S(2)}) collective-permute-start(bf16[384,512]{1,0:T(8,128)(2,1)S(1)} %get-tuple-element.29), channel_id=1, source_target_pairs={{0,2},{1,9},{2,0},{3,11},{4,6},{5,13},{6,4},{7,15},{8,10},{9,1},{1... | collective-permute-start | bytes 1179656 | tf_op jit(solution)/shard_map/ppermute | solution.py:248
  43.3 9.2 %collective-permute-start.7 = (bf16[384,512]{1,0:T(8,128)(2,1)S(1)}, bf16[384,512]{1,0:T(8,128)(2,1)S(1)}, u32[]{:S(2)}, u32[]{:S(2)}) collective-permute-start(bf16[384,512]{1,0:T(8,128)(2,1)S(1)} %get-tuple-element.30), channel_id=1, source_target_pairs={{0,8},{1,25},{2,10},{3,27},{4,12},{5,29},{6,14},{7,31},{8,0},{9,17... | collective-permute-start | bytes 1179656 | tf_op jit(solution)/shard_map/ppermute | solution.py:248
  43.8 0.7 %copy-start.5 = (bf16[2048,4]{0,1:T(4,128)(2,1)S(1)}, bf16[2048,4]{0,1:T(4,128)(2,1)}, u32[]{:S(2)}) copy-start(bf16[2048,4]{0,1:T(4,128)(2,1)} %param.6) | copy-start | bytes 49156
  43.8 2.3 %copy-start.4 = (s32[1,4,8]{2,1,0:T(4,128)S(1)}, s32[1,4,8]{2,1,0:T(4,128)}, u32[]{:S(2)}) copy-start(s32[1,4,8]{2,1,0:T(4,128)} %choices_ref.1) | copy-start | bytes 388
  44.8 1.3 %collective-permute-start.4 = (f32[128,4]{1,0:T(8,128)S(1)}, f32[128,4]{1,0:T(8,128)S(1)}, u32[]{:S(2)}, u32[]{:S(2)}) collective-permute-start(f32[128,4]{1,0:T(8,128)S(1)} %convolution_bitcast_fusion.logits_ref), channel_id=1, source_target_pairs={{0,1},{1,0},{2,3},{3,2},{4,5},{5,4},{6,7},{7,6},{8,9},{9,8},{10,11... | collective-permute-start | bytes 6152 | tf_op jit(solution)/shard_map/ppermute | solution.py:299
